TPU v7x, 256 devices: a whole 4x4x8 slice. The times are simulated.
256 devices in a mesh: tower: 8 (over x, y_hi), shard: 32 (over y_lo, z, core).
Axes of the slice: x: 4, y: 4 (y_hi: 2, y_lo: 2; y = y_hi * 2 + y_lo), z: 8, core: 2. Of those that a mesh axis runs over, the one named last changes fastest.
Arguments:
- pooled: bfloat16 [8, 512, 12800], P('tower', 'shard'), may hold values from -6 to 6
- dout: bfloat16 [512, 8, 512], P(('tower', 'shard')), may hold values from -6 to 6
- w_first: bfloat16 [8, 4096, 12800], P('tower', 'shard'), may hold values from -0.0546875 to 0.0546875
- w_second: bfloat16 [8, 4096, 512], P('tower', 'shard'), may hold values from -0.09375 to 0.09375
- table: float32 [8, 32768, 128], P('tower', 'shard'), may hold values from -6 to 6
- accum: float32 [8, 32768], P('tower', 'shard'), may hold values from 0.1 to 10
- touched_ids: int32 [8, 8192], P('tower', 'shard'), may hold values from 0 to 1023, as said below
- lookup_bag: int32 [8, 32, 32, 400], P('tower'), may hold values from 0 to 1599
- lookup_slot: int32 [8, 32, 32, 400], P('tower'), may hold values from 0 to 255
Outputs:
- grad_first: float32 [8, 4096, 12800], P('tower', 'shard')
- grad_second: float32 [8, 4096, 512], P('tower', 'shard')
- new_rows: float32 [8, 8192, 128], P('tower', 'shard')
- new_accum: float32 [8, 8192], P('tower', 'shard')
Inputs may be any that keep to these rules, and one draw needn't show every extreme that they name: `touched_ids`: the 256 row numbers of one device are distinct and include 0 and 1023.
All inputs are finite; a program needn't handle non-finite values.
Results may differ from a plain program's by a relative error of at most 0.0029.
Values may be sent and summed in bfloat16 or wider, within the bound.
A program may use at most 128 MiB of HBM per device.

v0:
```python
import jax
import jax.numpy as jnp
from jax import lax
from jax.sharding import PartitionSpec as P

EMB = 128
FEAT = 100
TOUCHED = 256


def contract_first(left, right):
    return lax.dot_general(
        left, right, (((0,), (0,)), ((), ())), preferred_element_type=jnp.float32
    )


def contract_last(left, right):
    return lax.dot_general(
        left, right, (((1,), (1,)), ((), ())), preferred_element_type=jnp.float32
    )


def row_sums(piece, bag_table, slot_table, sample_rows):
    count = piece.shape[0] // sample_rows
    flat = piece.reshape(count * sample_rows * FEAT, EMB)
    bags = bag_table
    bags = bags + (jnp.arange(count, dtype=jnp.int32) * (sample_rows * FEAT))[:, None]
    picked = flat[bags.reshape(-1)]
    onehot = (
        slot_table.reshape(-1)[:, None] == jnp.arange(TOUCHED, dtype=jnp.int32)[None, :]
    ).astype(jnp.bfloat16)
    return contract_first(onehot, picked)


def shards(pooled, dout, w_first, w_second, table, accum, touched_ids, lookup_bag, lookup_slot):
    arrived = lax.all_to_all(dout, "tower", split_axis=1, concat_axis=0, tiled=True)
    grad_out = arrived.reshape(arrived.shape[0], arrived.shape[2])
    inputs = pooled[0]
    sample_rows = inputs.shape[0]
    n_shard = lax.axis_size("shard")
    me_index = lax.axis_index("shard")
    scale = float(sample_rows * n_shard) ** (-0.5)
    inputs_all, grad_all = (
        lax.all_gather(inputs, "shard", axis=0, tiled=True),
        lax.all_gather(grad_out, "shard", axis=0, tiled=True),
    )
    pre = contract_last(inputs_all, w_first[0])
    sig = jax.nn.sigmoid(pre)
    hidden = (pre * sig).astype(jnp.bfloat16)
    back_hidden = contract_last(grad_all, w_second[0])
    back_pre = (back_hidden * sig * (1.0 + pre * (1.0 - sig))).astype(jnp.bfloat16)
    grad_first = contract_first(back_pre, inputs_all) * scale
    grad_second = contract_first(hidden, grad_all) * scale
    back_pooled = lax.psum_scatter(
        jnp.dot(back_pre, w_first[0], preferred_element_type=jnp.float32),
        "shard",
        scatter_dimension=0,
        tiled=True,
    ).astype(jnp.bfloat16)
    bag_table = lax.dynamic_index_in_dim(lookup_bag[0], me_index, 0, keepdims=False)
    slot_table = lax.dynamic_index_in_dim(lookup_slot[0], me_index, 0, keepdims=False)
    row_grad = row_sums(
        lax.all_gather(back_pooled, "shard", axis=0, tiled=True), bag_table, slot_table, sample_rows
    )
    row_ids = touched_ids[0]
    old_rows = table[0][row_ids]
    old_acc = accum[0][row_ids]
    new_acc = old_acc + jnp.mean(row_grad * row_grad, axis=-1)
    new_row = old_rows - 0.5 * row_grad / (jnp.sqrt(new_acc)[:, None] + 1e-08)
    return (grad_first[None], grad_second[None], new_row[None], new_acc[None])


def solution(mesh):
    in_specs = (
        P("tower", "shard", None),
        P(("tower", "shard"), None, None),
        P("tower", "shard", None),
        P("tower", "shard", None),
        P("tower", "shard", None),
        P("tower", "shard"),
        P("tower", "shard"),
        P("tower", None, None, None),
        P("tower", None, None, None),
    )
    out_specs = (
        P("tower", "shard", None),
        P("tower", "shard", None),
        P("tower", "shard", None),
        P("tower", "shard"),
    )
    return jax.shard_map(shards, mesh=mesh, in_specs=in_specs, out_specs=out_specs, check_vma=False)
```

profile of v0, /device:TPU:1, one launch (start us, length us, event | category | flops | bytes accessed | tf_op | source)
XLA Modules:
  0.0 433.2 jit_solution(15036396803353617242)
XLA Ops:
  7.2 0.7 all-gather.6.cloned.1.call-update
  7.9 0.0 reduce-scatter.2.cloned.1.call-start
  8.0 0.9 copy.18
  8.9 13.8 %all_to_all.15 = bf16[2,8,512]{2,0,1:T(2,128)(2,1)S(1)} all-to-all(bf16[2,8,512]{2,0,1:T(2,128)(2,1)S(1)} %copy.18), channel_id=1, replica_groups=mesh['tower'=8,'shard'=32] {'tower'}, dimensions={1} | all-to-all | bytes 32768 | tf_op jit(solution)/shard_map/all_to_all | solution.py:36
  22.7 43.2 %all_gather.9 = bf16[512,512]{1,0:T(8,128)(2,1)} all-gather(bf16[16,512]{1,0:T(8,128)(2,1)S(1)} %reshape.108), channel_id=1, replica_groups=mesh['tower'=8,'shard'=32] {'shard'}, dimensions={0}, use_global_device_ids=true | all-gather | bytes 540672 | tf_op jit(solution)/shard_map/all_gather | solution.py:45
  65.9 32.8 %all-gather.6.cloned.1.call-done = bf16[1,512,12800]{2,1,0:T(8,128)(2,1)} async-done(((bf16[1,16,12800]{2,1,0:T(8,128)(2,1)}), bf16[1,512,12800]{2,1,0:T(8,128)(2,1)}) %all-gather.6.cloned.1.call-update) | async-done | bytes 13107216 | tf_op jit(solution)/shard_map/all_gather | solution.py:44
  98.7 6.7 %fusion.2 = f32[512,128]{1,0:T(8,128)S(1)} fusion(bf16[1,512,12800]{2,1,0:T(8,128)(2,1)} %all-gather.6.cloned.1.call-done, bf16[1,128,12800]{2,1,0:T(8,128)(2,1)S(1)} %copy-done), kind=kOutput, calls=%fused_computation.6 | convolution fusion | flops 1677721600 | bytes 16646144 | tf_op jit(solution)/shard_map/dot_general | solution.py:18
  105.4 0.7 copy-done.10
  106.1 0.3 fusion.11
  106.4 10.6 %fusion.6 = f32[512,12800]{1,0:T(8,128)} fusion(bf16[512,128]{1,0:T(8,128)(2,1)S(1)} %fusion.11, bf16[1,128,12800]{2,1,0:T(8,128)(2,1)S(1)} %copy-done), kind=kOutput, calls=%fused_computation.11 | convolution fusion | flops 1677721600 | bytes 29622272 | tf_op jit(solution)/shard_map/dot_general | solution.py:55
  117.1 0.0 all-gather.4.cloned.1.call-start
  117.2 158.8 %reduce-scatter.2.cloned.1.call-done = f32[16,12800]{1,0:T(8,128)} async-done(((f32[512,12800]{1,0:T(8,128)}), f32[16,12800]{1,0:T(8,128)}) %reduce-scatter.2.cloned.1.call-update) | async-done | bytes 819216 | tf_op jit(solution)/shard_map/reduce_scatter | solution.py:54
  276.0 2.0 convert_element_type.12
  278.0 0.7 gather_fusion
  278.7 0.1 copy.19
  278.8 0.8 constant_dynamic-slice_fusion
  279.7 0.1 squeeze.31
  279.8 0.1 add.87
  279.9 0.1 add.88
  280.1 0.9 constant_dynamic-slice_fusion.1
  280.9 0.7 eq.15
  281.7 1.4 gather_fusion.2
  283.0 0.2 fusion.14
  283.2 0.6 pad_clamp_fusion
  283.8 1.0 fusion.9
  284.8 9.8 %fusion = f32[1,128,12800]{2,1,0:T(8,128)} fusion(bf16[512,128]{1,0:T(8,128)(2,1)S(1)} %fusion.11, bf16[1,512,12800]{2,1,0:T(8,128)(2,1)} %all-gather.6.cloned.1.call-done), kind=kOutput, calls=%fused_computation.4 | convolution fusion | flops 1679360000 | bytes 19791872 | tf_op jit(solution)/shard_map/dot_general | solution.py:12
  294.6 63.9 %all-gather.4.cloned.1.call-done = bf16[512,12800]{1,0:T(8,128)(2,1)} async-done(((bf16[16,12800]{1,0:T(8,128)(2,1)}), bf16[512,12800]{1,0:T(8,128)(2,1)}) %all-gather.4.cloned.1.call-update) | async-done | bytes 13107216 | tf_op jit(solution)/shard_map/all_gather | solution.py:63
  358.5 26.4 %reshape.109 = bf16[51200,128]{1,0:T(8,128)(2,1)} reshape(bf16[512,12800]{1,0:T(8,128)(2,1)} %all-gather.4.cloned.1.call-done) | data formatting | bytes 26214400 | tf_op jit(solution)/shard_map/reshape | solution.py:25
  385.0 30.8 %gather_fusion.1 = bf16[12800,128]{1,0:T(8,128)(2,1)} fusion(bf16[51200,128]{1,0:T(8,128)(2,1)} %reshape.109, s32[13312]{0:T(1024)S(1)} %copy-done.6), kind=kCustom, calls=%fused_computation.1 | custom fusion | bytes 6604800 | tf_op jit(solution)/shard_map/gather | solution.py:28
  415.8 9.5 %multiply_reduce_fusion = (f32[256]{0:T(256)S(1)}, f32[256,128]{0,1:T(8,128)S(1)}) fusion(bf16[12800,128]{1,0:T(8,128)(2,1)} %gather_fusion.1, s32[12800]{0:T(1024)S(1)} %copy-done.7), kind=kOutput, calls=%fused_computation.24 | convolution fusion | flops 842202880 | bytes 3460096 | tf_op jit(solution)/shard_map/dot_general | solution.py:12
  425.4 0.6 sqrt_add_fusion
  426.0 0.8 copy.20
  (31 shorter events, 0.2 us)
Async XLA Ops:
  7.2 91.6 %copy-start = (bf16[1,128,12800]{2,1,0:T(8,128)(2,1)S(1)}, bf16[1,128,12800]{2,1,0:T(8,128)(2,1)}, u32[]{:S(2)}) copy-start(bf16[1,128,12800]{2,1,0:T(8,128)(2,1)} %param.11) | copy-start | bytes 9830404
  7.2 91.5 %all-gather.6.cloned.1.call-start = ((), (), s32[]{:S(2)}) async-start(), calls=%async_computation.4 | async-start | bytes 13516800 | tf_op jit(solution)/shard_map/all_gather | solution.py:44
  7.9 268.0 %reduce-scatter.2.cloned.1.call-start = ((), (), s32[]{:S(2)}) async-start(), calls=%async_computation.2 | async-start | bytes 27033600 | tf_op jit(solution)/shard_map/reduce_scatter | solution.py:54
  65.9 40.2 %copy-start.9 = (bf16[1,128,512]{2,1,0:T(8,128)(2,1)S(1)}, bf16[1,128,512]{2,1,0:T(8,128)(2,1)}, u32[]{:S(2)}) copy-start(bf16[1,128,512]{2,1,0:T(8,128)(2,1)} %param.12) | copy-start | bytes 393220
  98.7 7.4 %copy-start.4 = (bf16[512,512]{1,0:T(8,128)(2,1)S(1)}, bf16[512,512]{1,0:T(8,128)(2,1)}, u32[]{:S(2)}) copy-start(bf16[512,512]{1,0:T(8,128)(2,1)} %all_gather.9) | copy-start | bytes 1572868
  105.4 0.7 copy-start.10
  117.0 160.9 %copy-start.8 = (s32[1,256]{1,0:T(1,128)S(1)}, s32[1,256]{1,0:T(1,128)}, u32[]{:S(2)}) copy-start(s32[1,256]{1,0:T(1,128)} %param.15) | copy-start | bytes 3076
  117.0 160.9 %copy-start.3 = (f32[1,1024,128]{2,1,0:T(8,128)S(1)}, f32[1,1024,128]{2,1,0:T(8,128)}, u32[]{:S(2)}) copy-start(f32[1,1024,128]{2,1,0:T(8,128)} %param.13) | copy-start | bytes 1572868
  117.1 164.6 %copy-start.2 = (f32[1,1024]{1,0:T(1,128)S(1)}, f32[1,1024]{1,0:T(1,128)}, u32[]{:S(2)}) copy-start(f32[1,1024]{1,0:T(1,128)} %param.14) | copy-start | bytes 12292
  117.1 166.8 %copy-start.5 = (bf16[512,512]{1,0:T(8,128)(2,1)S(1)}, bf16[512,512]{1,0:T(8,128)(2,1)}, u32[]{:S(2)}) copy-start(bf16[512,512]{1,0:T(8,128)(2,1)} %all_gather.9) | copy-start | bytes 1572868
  117.1 166.7 %copy-start.11 = (f32[512,128]{1,0:T(8,128)S(1)}, f32[512,128]{1,0:T(8,128)}, u32[]{:S(2)}) copy-start(f32[512,128]{1,0:T(8,128)} %copy-done.10) | copy-start | bytes 786436
  117.1 241.4 %all-gather.4.cloned.1.call-start = ((), (), s32[]{:S(2)}) async-start(), calls=%async_computation.3 | async-start | bytes 13516800 | tf_op jit(solution)/shard_map/all_gather | solution.py:63
  294.6 90.4 %copy-start.6 = (s32[13312]{0:T(1024)S(1)}, s32[13312]{0:T(1024)}, u32[]{:S(2)}) copy-start(s32[13312]{0:T(1024)} %pad_clamp_fusion) | copy-start | bytes 159748
  385.0 30.9 %copy-start.7 = (s32[12800]{0:T(1024)S(1)}, s32[12800]{0:T(1024)}, u32[]{:S(2)}) copy-start(s32[12800]{0:T(1024)} %eq.15) | copy-start | bytes 153604
  385.0 41.8 %copy-start.1 = (bf16[1,128,12800]{2,1,0:T(8,128)(2,1)S(1)}, bf16[1,128,12800]{2,1,0:T(8,128)(2,1)}, u32[]{:S(2)}) copy-start(bf16[1,128,12800]{2,1,0:T(8,128)(2,1)} %param.11) | copy-start | bytes 9830404
Sparse Core Ops, SparseCore 0:
  9.9 88.8 all-gather.5
  117.2 158.7 reduce-scatter.1
  278.1 80.4 all-gather.3
where the time goes:
time: 434 us; the launch traced here: 433 us
  waiting for transfers between devices  256 us (59%)
  local copies, waits for them, and re-layouts  64.7 us (15%)
  blocking collectives  57 us (13%)
  matrix products  37.9 us (9%)
  between operations  13.9 us (3%)
    reduce_scatter x1, waiting for transfers between devices, shards(): lax.psum_scatter(jnp.dot(back_pre, w_first[0], preferred_element_type=jnp...  159 us
    all_gather x1, waiting for transfers between devices, shards(): lax.all_gather(back_pooled, 'shard', axis=0, tiled=True)  63.9 us
    all_gather x1, blocking collectives, shards(): lax.all_gather(grad_out, 'shard', axis=0, tiled=True)  43.2 us
    all_gather x1, waiting for transfers between devices, shards(): lax.all_gather(inputs, 'shard', axis=0, tiled=True)  32.8 us
    gather x1, local copies, waits for them, and re-layouts, row_sums(): picked = flat[bags.reshape(-1)]  30.8 us
    reshape x1, local copies, waits for them, and re-layouts, row_sums(): flat = piece.reshape(count * sample_rows * FEAT, EMB)  26.4 us
    dot_general x3, matrix products, contract_first(): lax.dot_general(left, right, (((0,), (0,)), ((), ())), preferred_element_...  20.3 us
    all_to_all x1, blocking collectives, shards(): lax.all_to_all(dout, 'tower', split_axis=1, concat_axis=0, tiled=True)  13.8 us
  transfers between devices with their start and end apart: 3, of which 3 were waited for; matrix products, arithmetic and copies ran while one was open for 4% of the time, Pallas kernels for 0%

commit v1 on v0

v1 whole, which is shorter than its diff:
```python
import jax
import jax.numpy as jnp
from jax import lax
from jax.experimental import pallas as pl
from jax.experimental.pallas import tpu as pltpu
from jax.sharding import PartitionSpec as P

EMB = 128
FEAT = 100
TOUCHED = 256
MESH = pl.DeviceIdType.MESH
VMEM = pltpu.VMEM
DMA = pltpu.SemaphoreType.DMA
NZ = 8
BF = jnp.bfloat16
F32 = jnp.float32


def contract_first(left, right):
    return lax.dot_general(left, right, (((0,), (0,)), ((), ())), preferred_element_type=F32)


def contract_last(left, right):
    return lax.dot_general(left, right, (((1,), (1,)), ((), ())), preferred_element_type=F32)


def place():
    s = lax.axis_index("shard")
    return s, s // 16, (s // 2) % NZ, s % 2


def shard_of(y, z, c):
    return y * 16 + z * 2 + c


def shard_id(s):
    return {"shard": s}


def remote(src, dst, send, recv, where):
    return pltpu.make_async_remote_copy(
        src_ref=src, dst_ref=dst, send_sem=send, recv_sem=recv, device_id=where, device_id_type=MESH
    )


def gather_kernel(
    pooled, w, dout, bags, slots,
    big, gall, wq, counts,
    bag_v, slot_v, dgot, gown, stage,
    in_sem, dsend, drecv, loc_sem, out_sem,
    first_send, first_recv, ring_send, ring_recv, mate_send, mate_recv, wsend, wrecv,
):
    t = lax.axis_index("tower")
    s, y, z, c = place()
    towers = dout.shape[0]
    cols = pooled.shape[1]
    quarter = wq.shape[1]
    half = cols // 2
    mate, other, diag = shard_of(y, z, 1 - c), shard_of(1 - y, z, c), shard_of(1 - y, z, 1 - c)
    ahead, behind = shard_of(y, (z + 1) % NZ, c), shard_of(y, (z + NZ - 1) % NZ, c)

    load_bags = pltpu.make_async_copy(bags, bag_v, in_sem.at[0])
    load_slots = pltpu.make_async_copy(slots, slot_v, in_sem.at[1])
    load_bags.start()
    load_slots.start()

    barrier = pltpu.get_barrier_semaphore()
    for peer in (mate, other, diag, ahead, behind):
        pl.semaphore_signal(barrier, inc=1, device_id=shard_id(peer), device_id_type=MESH)
    for step in range(1, towers):
        pl.semaphore_signal(barrier, inc=1, device_id={"tower": (t + step) % towers}, device_id_type=MESH)
    pl.semaphore_wait(barrier, 5 + towers - 1)

    sent = []

    def block(zz, yy):
        return zz * 4 + yy * 2 + c

    def go(copy):
        copy.start()
        sent.append(copy)
        return copy

    mine = block(z, y)
    tile_rows = dout.shape[1]
    land = dgot.at[pl.ds(pl.multiple_of(t * tile_rows, tile_rows), tile_rows), :]
    dcopies = []
    for step in range(1, towers):
        u = (t + step) % towers
        dcopies.append(go(remote(dout.at[u], land, dsend.at[step], drecv.at[step], {"tower": u})))
    own_d = pltpu.make_async_copy(dout.at[t], land, loc_sem.at[0])
    own_d.start()

    firsts = []
    for i, peer in enumerate((ahead, behind, other)):
        firsts.append(go(remote(pooled, big.at[mine], first_send.at[0, i], first_recv.at[0, i], shard_id(peer))))
    mates = [go(remote(pooled, big.at[mine], mate_send.at[0, 0], mate_recv.at[0, 0], shard_id(mate)))]
    own_p = pltpu.make_async_copy(pooled, big.at[mine], loc_sem.at[1])
    own_p.start()

    own_d.wait()
    for copy in dcopies:
        copy.wait_recv()
    per = gown.shape[1] // EMB
    rows = gown.shape[0]
    for k in range(per):
        gown[:, k * EMB:(k + 1) * EMB] = dgot[pl.ds(k, rows, stride=per), :].astype(BF)
    for i, peer in enumerate((ahead, behind, other)):
        firsts.append(go(remote(gown, gall.at[mine], first_send.at[1, i], first_recv.at[1, i], shard_id(peer))))
    mates.append(go(remote(gown, gall.at[mine], mate_send.at[1, 0], mate_recv.at[1, 0], shard_id(mate))))
    own_g = pltpu.make_async_copy(gown, gall.at[mine], loc_sem.at[2])
    own_g.start()

    def view(kind, at):
        if kind == 0:
            return big.at[at]
        if kind == 1:
            return gall.at[at]
        return big.at[at, :, pl.ds((kind - 2) * half, half)]

    mate_slot = [1, 1]

    def to_mate(kind, at):
        row = 1 if kind == 1 else 0
        slot = mate_slot[row]
        mate_slot[row] += 1
        mates.append(go(remote(view(kind, at), view(kind, at), mate_send.at[row, slot], mate_recv.at[row, slot], shard_id(mate))))

    ring = {}

    def to_ring(kind, at, hop, direction, chain):
        row = 1 if kind == 1 else 0
        peer = behind if direction else ahead
        index = (hop - 1) * 4 + direction * 2 + chain
        ring[(row, hop, direction, chain)] = go(remote(
            view(kind, at), view(kind, at), ring_send.at[row, index], ring_recv.at[row, index], shard_id(peer)))

    yblock = block(z, 1 - y)
    firsts[2].wait_recv()
    for direction in range(2):
        to_ring(0, yblock, 1, direction, 1)
    to_mate(0, yblock)
    firsts[5].wait_recv()
    for direction in range(2):
        to_ring(1, yblock, 1, direction, 1)
    to_mate(1, yblock)

    hid = w.shape[0]
    me4 = y * 2 + c
    wcopies = []
    for i, (yy, cc, peer) in enumerate(((y, 1 - c, mate), (1 - y, c, other), (1 - y, 1 - c, diag))):
        part = pl.multiple_of((yy * 2 + cc) * quarter, EMB)
        wcopies.append(go(remote(
            w.at[:, pl.ds(part, quarter)], wq.at[pl.ds(pl.multiple_of(me4 * hid, hid), hid), :],
            wsend.at[i], wrecv.at[i], shard_id(peer))))
    own_w = pltpu.make_async_copy(
        w.at[:, pl.ds(pl.multiple_of(me4 * quarter, EMB), quarter)],
        wq.at[pl.ds(pl.multiple_of(me4 * hid, hid), hid), :], loc_sem.at[3])
    own_w.start()

    load_bags.wait()
    load_slots.wait()
    look = bags.shape[2]
    pad = stage.shape[2] // 4
    local_feat = quarter // EMB
    samples = pooled.shape[0]
    low = me4 * local_feat

    def owner_counts(owner, slot_at):
        @pl.when(owner >= 2)
        def _():
            pltpu.make_async_copy(stage.at[slot_at], counts.at[owner], out_sem.at[slot_at]).wait()

        for i in range(4):
            source = shard_of(i // 2, z, i % 2)
            bag = bag_v[owner, pl.ds(source, 1), :]
            slot = slot_v[owner, pl.ds(source, 1), :]
            sample = (bag * 5243) >> 19
            feat = bag - sample * FEAT - low
            ok = (feat >= 0) & (feat < local_feat)
            bag_local = jnp.where(ok, feat * samples + sample, -1)
            left = (lax.broadcasted_iota(jnp.int32, (TOUCHED, look), 0) == slot).astype(F32).astype(BF)
            right = (lax.broadcasted_iota(jnp.int32, (pad, look), 0) == bag_local).astype(F32).astype(BF)
            stage[slot_at, :, i * pad:(i + 1) * pad] = contract_last(left, right).astype(BF)
        pltpu.make_async_copy(stage.at[slot_at], counts.at[owner], out_sem.at[slot_at]).start()

    owners = bags.shape[0]
    done = [0]

    def count_some(pairs):
        start = done[0]
        done[0] += pairs

        def body(p, carry):
            owner_counts(p * 2, 0)
            owner_counts(p * 2 + 1, 1)
            return carry

        lax.fori_loop(start, start + pairs, body, 0)

    count_some(4)
    for hop in range(1, 4):
        for chain in range(2):
            count_some(2)
            yy = y if chain == 0 else 1 - y
            for direction in range(2):
                zz = (z + hop) % NZ if direction else (z + NZ - hop) % NZ
                at = block(zz, yy)
                if hop == 1 and chain == 0:
                    firsts[direction].wait_recv()
                else:
                    ring[(0, hop, direction, chain)].wait_recv()
                to_ring(0 if hop < 3 else 2 + direction, at, hop + 1, direction, chain)
                to_mate(0, at)
                if hop == 1 and chain == 0:
                    firsts[3 + direction].wait_recv()
                else:
                    ring[(1, hop, direction, chain)].wait_recv()
                if hop < 3 or direction == 0:
                    to_ring(1, at, hop + 1, direction, chain)
                to_mate(1, at)
    zz = (z + 4) % NZ
    for chain in range(2):
        yy = y if chain == 0 else 1 - y
        at = block(zz, yy)
        for direction in range(2):
            ring[(0, 4, direction, chain)].wait_recv()
            to_mate(2 + direction, at)
        ring[(1, 4, 0, chain)].wait_recv()
        to_mate(1, at)
    for copy in mates:
        copy.wait_recv()
    for copy in wcopies:
        copy.wait_recv()
    for copy in sent:
        copy.wait_send()
    for copy in (own_p, own_g, own_w):
        copy.wait()
    for slot_at in range(2):
        pltpu.make_async_copy(stage.at[slot_at], counts.at[owners - 2 + slot_at], out_sem.at[slot_at]).wait()


def gather_all(pooled, w, dout, bags, slots):
    samples, cols = pooled.shape
    hid = w.shape[0]
    out = dout.shape[1] * EMB * dout.shape[0] // samples
    n_shard = bags.shape[0]
    quarter = cols // 4
    local = quarter // EMB * samples
    pad = -(-local // 128) * 128
    pad = max(pad, 512) if local > 256 else pad
    any_spec = pl.BlockSpec(memory_space=pl.ANY)
    return pl.pallas_call(
        gather_kernel,
        out_shape=(
            jax.ShapeDtypeStruct((n_shard, samples, cols), BF),
            jax.ShapeDtypeStruct((n_shard, samples, out), BF),
            jax.ShapeDtypeStruct((4 * hid, quarter), BF),
            jax.ShapeDtypeStruct((n_shard, TOUCHED, 4 * pad), BF),
        ),
        in_specs=[any_spec] * 5,
        out_specs=(any_spec,) * 4,
        scratch_shapes=[
            VMEM(bags.shape, jnp.int32),
            VMEM(slots.shape, jnp.int32),
            VMEM((dout.shape[0] * dout.shape[1], EMB), F32),
            VMEM((samples, out), BF),
            VMEM((2, TOUCHED, 4 * pad), BF),
            DMA((2,)), DMA((8,)), DMA((8,)), DMA((4,)), DMA((2,)),
            DMA((2, 3)), DMA((2, 3)), DMA((2, 16)), DMA((2, 16)), DMA((2, 18)), DMA((2, 18)), DMA((3,)), DMA((3,)),
        ],
        compiler_params=pltpu.CompilerParams(
            collective_id=0, has_side_effects=True, vmem_limit_bytes=48 * 1024 * 1024
        ),
        name="gather",
    )(pooled, w, dout, bags, slots)


def reduce_kernel(
    bp, wq, flat,
    bpall, first, up_send, down_send, up_recv, down_recv, acc,
    bsend, brecv, fsend, frecv, usend, urecv, vsend, vrecv,
):
    s, y, z, c = place()
    mate, other, diag = shard_of(y, z, 1 - c), shard_of(1 - y, z, c), shard_of(1 - y, z, 1 - c)
    ahead, behind = shard_of(y, (z + 1) % NZ, c), shard_of(y, (z + NZ - 1) % NZ, c)
    hid = bp.shape[1]
    quarter = wq.shape[1]
    rows = acc.shape[1]
    cut = (quarter // EMB + 1) // 2 * EMB
    barrier = pltpu.get_barrier_semaphore()
    peers = (mate, other, diag, ahead, behind)
    for peer in peers:
        pl.semaphore_signal(barrier, inc=1, device_id=shard_id(peer), device_id_type=MESH)
    pl.semaphore_wait(barrier, len(peers))
    me4 = pl.multiple_of((y * 2 + c) * hid, hid)
    sent = []

    def go(copy):
        copy.start()
        sent.append(copy)
        return copy

    got = [
        go(remote(bp, bpall.at[:, pl.ds(me4, hid)], bsend.at[i], brecv.at[i], shard_id(peer)))
        for i, peer in enumerate((other, diag, mate))
    ]
    bpall[:, pl.ds(me4, hid)] = bp[...]
    for copy in got:
        copy.wait_recv()

    tile = quarter // 5 if quarter % (5 * EMB) == 0 else EMB
    tiles = quarter // tile

    def product(slab, write):
        left = bpall[pl.ds(pl.multiple_of(slab * rows, rows), rows), :]

        def body(i, carry):
            at = pl.multiple_of(i * tile, EMB)
            write(at, jnp.dot(left, wq[:, pl.ds(at, tile)], preferred_element_type=F32))
            return carry

        lax.fori_loop(0, tiles, body, 0)

    def into_first(at, value):
        first[:, pl.ds(at, tile)] = value.astype(BF)

    def into_acc(which):
        def write(at, value):
            acc[which, :, pl.ds(at, tile)] = value
        return write

    product((z + 4) % NZ, into_first)
    arriving = [
        go(remote(first.at[:, :cut], up_recv.at[0, :, pl.ds(0, cut)], fsend.at[0], frecv.at[0], shard_id(ahead))),
        go(remote(first.at[:, cut:], down_recv.at[0, :, pl.ds(cut, quarter - cut)], fsend.at[1], frecv.at[1], shard_id(behind))),
    ]
    for k in range(3):
        hop = 3 - k
        product((z + hop) % NZ, into_acc(0))
        product((z + NZ - hop) % NZ, into_acc(1))
        arriving[0].wait_recv()
        if k == 0:
            up_send[k, :, :cut] = (acc[0, :, :cut] + up_recv[k, :, :cut].astype(F32)).astype(BF)
            up_send[k, :, cut:] = acc[0, :, cut:].astype(BF)
        else:
            up_send[k] = (acc[0] + up_recv[k].astype(F32)).astype(BF)
        up = go(remote(up_send.at[k], up_recv.at[k + 1], usend.at[k], urecv.at[k], shard_id(ahead)))
        arriving[1].wait_recv()
        if k == 0:
            down_send[k, :, cut:] = (acc[1, :, cut:] + down_recv[k, :, cut:].astype(F32)).astype(BF)
            down_send[k, :, :cut] = acc[1, :, :cut].astype(BF)
        else:
            down_send[k] = (acc[1] + down_recv[k].astype(F32)).astype(BF)
        down = go(remote(down_send.at[k], down_recv.at[k + 1], vsend.at[k], vrecv.at[k], shard_id(behind)))
        arriving = [up, down]
    product(z, into_acc(0))
    flat[...] = jnp.zeros_like(flat)
    for copy in arriving:
        copy.wait_recv()
    samples = rows // 4
    for f in range(quarter // EMB):
        at = slice(f * EMB, (f + 1) * EMB)
        total = acc[0, :, at] + up_recv[3, :, at].astype(F32) + down_recv[3, :, at].astype(F32)
        total = total.astype(BF)
        for i in range(4):
            flat[i, f * samples:(f + 1) * samples, :] = total[i * samples:(i + 1) * samples]
    for copy in sent:
        copy.wait_send()


def reduce_all(bp, wq, pad, samples):
    batch, hid = bp.shape
    quarter = wq.shape[1]
    rows = 4 * samples
    vm = pl.BlockSpec(memory_space=VMEM)
    return pl.pallas_call(
        reduce_kernel,
        out_shape=jax.ShapeDtypeStruct((4, pad, EMB), BF),
        in_specs=[vm, vm],
        out_specs=vm,
        scratch_shapes=[
            VMEM((batch, 4 * hid), BF),
            VMEM((rows, quarter), BF),
            VMEM((3, rows, quarter), BF),
            VMEM((3, rows, quarter), BF),
            VMEM((4, rows, quarter), BF),
            VMEM((4, rows, quarter), BF),
            VMEM((2, rows, quarter), F32),
            DMA((3,)), DMA((3,)), DMA((2,)), DMA((2,)), DMA((3,)), DMA((3,)), DMA((3,)), DMA((3,)),
        ],
        compiler_params=pltpu.CompilerParams(
            collective_id=1, has_side_effects=True, vmem_limit_bytes=48 * 1024 * 1024
        ),
        name="reduce",
    )(bp, wq)


def shards(pooled, dout, w_first, w_second, table, accum, touched_ids, lookup_bag, lookup_slot):
    towers = dout.shape[1]
    samples = pooled.shape[1]
    dtiles = jnp.transpose(dout, (1, 0, 2)).astype(F32).reshape(towers, -1, EMB)
    big, gall, wq, counts = gather_all(pooled[0], w_first[0], dtiles, lookup_bag[0], lookup_slot[0])
    n_shard = big.shape[0]
    inputs_all = big.reshape(n_shard * samples, -1)
    grad_all = gall.reshape(n_shard * samples, -1)
    scale = float(samples * n_shard) ** (-0.5)
    pre = contract_last(inputs_all, w_first[0])
    sig = jax.nn.sigmoid(pre)
    hidden = (pre * sig).astype(BF)
    back_hidden = contract_last(grad_all, w_second[0])
    back_pre = (back_hidden * sig * (1.0 + pre * (1.0 - sig))).astype(BF)
    flat = reduce_all(back_pre, wq, counts.shape[2] // 4, samples)
    partial = jnp.dot(
        counts.reshape(n_shard * TOUCHED, -1), flat.reshape(-1, EMB), preferred_element_type=F32
    )
    row_grad = lax.psum_scatter(partial, "shard", scatter_dimension=0, tiled=True)
    grad_first = contract_first(back_pre, inputs_all) * scale
    grad_second = contract_first(hidden, grad_all) * scale
    row_ids = touched_ids[0]
    old_rows = table[0][row_ids]
    old_acc = accum[0][row_ids]
    new_acc = old_acc + jnp.mean(row_grad * row_grad, axis=-1)
    new_row = old_rows - 0.5 * row_grad / (jnp.sqrt(new_acc)[:, None] + 1e-08)
    return (grad_first[None], grad_second[None], new_row[None], new_acc[None])


def solution(mesh):
    in_specs = (
        P("tower", "shard", None),
        P(("tower", "shard"), None, None),
        P("tower", "shard", None),
        P("tower", "shard", None),
        P("tower", "shard", None),
        P("tower", "shard"),
        P("tower", "shard"),
        P("tower", None, None, None),
        P("tower", None, None, None),
    )
    out_specs = (
        P("tower", "shard", None),
        P("tower", "shard", None),
        P("tower", "shard", None),
        P("tower", "shard"),
    )
    return jax.shard_map(shards, mesh=mesh, in_specs=in_specs, out_specs=out_specs, check_vma=False)
```

time: 434 us -> 295 us (0.68)
  waiting for transfers between devices: 256 us -> 103 us
  Pallas kernels: 0 us -> 129 us
  local copies, waits for them, and re-layouts: 64.7 us -> 6.37 us
  blocking collectives: 57 us -> 0 us
    pallas_call x0 -> x2, Pallas kernels: none -> 129 us  [the longest x1 83.8 us: gather_all(): pl.pallas_call(gather_kernel, out_shape=(jax.ShapeDtypeStruct((n_shard, s...]
    all_gather x2 -> x0, waiting for transfers between devices: 96.7 us -> none  [the longest x1 63.9 us: shards(): lax.all_gather(back_pooled, 'shard', axis=0, tiled=True)]
    reduce_scatter x1, waiting for transfers between devices: 159 us -> 103 us  [shards(): lax.psum_scatter(partial, 'shard', scatter_dimension=0, tiled=True)]
    all_gather x1 -> x0, blocking collectives: 43.2 us -> none  [shards(): lax.all_gather(grad_out, 'shard', axis=0, tiled=True)]
    gather x1 -> x0, local copies, waits for them, and re-layouts: 30.8 us -> none  [row_sums(): picked = flat[bags.reshape(-1)]]
    reshape x2, local copies, waits for them, and re-layouts: 26.4 us -> 0.06 us  [shards(): dtiles = jnp.transpose(dout, (1, 0, 2)).astype(F32).reshape(towers, -1, EMB)]
    all_to_all x1 -> x0, blocking collectives: 13.8 us -> none  [shards(): lax.all_to_all(dout, 'tower', split_axis=1, concat_axis=0, tiled=True)]
    dot_general x3 -> x2, matrix products: 20.3 us -> 10.5 us  [contract_first(): lax.dot_general(left, right, (((0,), (0,)), ((), ())), preferred_element_...]
  transfers between devices with their start and end apart: 3 -> 1, of which waited for: 3 -> 1; matrix products, arithmetic and copies ran while one was open for 4% -> 4% of each run, Pallas kernels for 0% -> 0%
where the time goes in v1:
time: 295 us; the launch traced here: 292 us
  Pallas kernels  129 us (44%)
  waiting for transfers between devices  103 us (35%)
  matrix products  34.6 us (12%)
  between operations  14.2 us (5%)
  local copies, waits for them, and re-layouts  6.37 us (2%)
  other arithmetic  4.03 us (1%)
    reduce_scatter x1, waiting for transfers between devices, shards(): lax.psum_scatter(partial, 'shard', scatter_dimension=0, tiled=True)  103 us
    pallas_call x1, Pallas kernels, gather_all(): pl.pallas_call(gather_kernel, out_shape=(jax.ShapeDtypeStruct((n_shard, s...  83.8 us
    pallas_call x1, Pallas kernels, reduce_all(): pl.pallas_call(reduce_kernel, out_shape=jax.ShapeDtypeStruct((4, pad, EMB...  45.3 us
    dot_general x1, matrix products, shards(): jnp.dot(counts.reshape(n_shard * TOUCHED, -1), flat.reshape(-1, EMB), pre...  17.1 us
    dot_general x2, matrix products, contract_first(): lax.dot_general(left, right, (((0,), (0,)), ((), ())), preferred_element_...  10.5 us
    dot_general x2, matrix products, contract_last(): lax.dot_general(left, right, (((1,), (1,)), ((), ())), preferred_element_...  7.05 us
  transfers between devices with their start and end apart: 1, of which 1 were waited for; matrix products, arithmetic and copies ran while one was open for 4% of the time, Pallas kernels for 0%

profile of v1, /device:TPU:1, one launch (start us, length us, event | category | flops | bytes accessed | tf_op | source)
XLA Modules:
  0.0 291.6 jit_solution(8126441267899364093)
XLA Ops:
  7.2 0.0 copy-start
  7.2 0.0 reduce-scatter.2.cloned.1.call-start
  7.2 0.8 convert_bitcast_fusion
  8.1 0.0 copy-start.2
  8.1 1.6 copy-done.2
  9.7 0.0 copy-start.3
  9.7 1.6 copy-done.3
  11.3 1.0 copy-done.4
  12.3 83.8 %gather.13 = (bf16[32,16,12800]{2,1,0:T(8,128)(2,1)}, bf16[32,16,512]{2,1,0:T(8,128)(2,1)S(1)}, bf16[512,3200]{1,0:T(8,128)(2,1)}, bf16[32,256,2048]{2,1,0:T(8,128)(2,1)}) custom-call(bf16[16,12800]{1,0:T(8,128)(2,1)S(1)} %bitcast.38, bf16[128,12800]{1,0:T(8,128)(2,1)} %bitcast.44, f32[8,8,128]{2,1,0:T(8,128)S(1)} %reshape.86.dout, ...), custom_call_target="tpu_custom_call" | custom-call | tf_op jit(solution)/shard_map/gather/pallas_call | solution.py:253
  96.0 0.0 copy-done.6
  96.0 0.0 copy-start.8
  96.1 0.0 copy-start.1
  96.1 6.7 %fusion.6 = f32[512,128]{1,0:T(8,128)S(1)} fusion(bf16[512,12800]{1,0:T(8,128)(2,1)} %bitcast.42, bf16[1,128,12800]{2,1,0:T(8,128)(2,1)S(1)} %copy-done.6), kind=kOutput, calls=%fused_computation.20 | convolution fusion | flops 1677721600 | bytes 16646144 | tf_op jit(solution)/shard_map/dot_general | solution.py:24
  102.8 0.0 copy-done.8
  102.8 0.3 fusion.3.bp
  103.1 0.0 copy-done.1
  103.1 45.3 %reduce.1 = bf16[4,512,128]{2,1,0:T(8,128)(2,1)S(1)} custom-call(bf16[512,128]{1,0:T(8,128)(2,1)S(1)} %fusion.3.bp, bf16[512,3200]{1,0:T(8,128)(2,1)S(1)} %copy-done.1), custom_call_target="tpu_custom_call" | custom-call | tf_op jit(solution)/shard_map/reduce/pallas_call | solution.py:377
  148.5 0.0 copy-start.7
  148.5 0.0 copy-start.5
  148.5 17.1 %fusion.9 = f32[8192,128]{1,0:T(8,128)} fusion(bf16[8192,2048]{1,0:T(8,128)(2,1)} %bitcast.47, bf16[2048,128]{1,0:T(8,128)(2,1)S(1)} %bitcast.37), kind=kOutput, calls=%fused_computation.23 | convolution fusion | flops 4294967296 | bytes 38273024 | tf_op jit(solution)/shard_map/dot_general | solution.py:414
  165.6 0.0 reduce-scatter.2.cloned.1.call-update
  165.6 0.0 copy-done.7
  165.6 0.0 copy-done.5
  165.6 1.4 gather_fusion.1
  167.0 0.0 copy-done
  167.0 0.7 gather_fusion
  167.8 1.0 fusion.1
  168.7 9.5 %fusion = f32[1,128,12800]{2,1,0:T(8,128)} fusion(bf16[512,128]{1,0:T(8,128)(2,1)S(1)} %fusion.3.bp, bf16[512,12800]{1,0:T(8,128)(2,1)} %bitcast.43), kind=kOutput, calls=%fused_computation.3 | convolution fusion | flops 1679360000 | bytes 19791872 | tf_op jit(solution)/shard_map/dot_general | solution.py:20
  178.2 103.2 %reduce-scatter.2.cloned.1.call-done = f32[256,128]{1,0:T(8,128)} async-done(((f32[8192,128]{1,0:T(8,128)}), f32[256,128]{1,0:T(8,128)}) %reduce-scatter.2.cloned.1.call-update) | async-done | bytes 131088 | tf_op jit(solution)/shard_map/reduce_scatter | solution.py:417
  281.5 1.0 multiply_reduce_fusion
  282.5 0.6 sqrt_add_fusion
  283.1 1.7 subtract_bitcast_fusion
  (6 shorter events, 0.1 us)
Async XLA Ops:
  7.2 159.9 %copy-start = (f32[1,1024,128]{2,1,0:T(8,128)S(1)}, f32[1,1024,128]{2,1,0:T(8,128)}, u32[]{:S(2)}) copy-start(f32[1,1024,128]{2,1,0:T(8,128)} %param.13) | copy-start | bytes 1572868
  7.2 274.3 %reduce-scatter.2.cloned.1.call-start = ((), (), s32[]{:S(2)}) async-start(), calls=%async_computation.1 | async-start | bytes 4325376 | tf_op jit(solution)/shard_map/reduce_scatter | solution.py:417
  8.1 1.6 copy-start.2
  9.7 1.6 copy-start.3
  11.2 1.0 copy-start.4
  12.3 83.8 %copy-start.6 = (bf16[1,128,12800]{2,1,0:T(8,128)(2,1)S(1)}, bf16[1,128,12800]{2,1,0:T(8,128)(2,1)}, u32[]{:S(2)}) copy-start(bf16[1,128,12800]{2,1,0:T(8,128)(2,1)} %param.11) | copy-start | bytes 9830404
  96.0 6.8 %copy-start.8 = (bf16[1,128,512]{2,1,0:T(8,128)(2,1)S(1)}, bf16[1,128,512]{2,1,0:T(8,128)(2,1)}, u32[]{:S(2)}) copy-start(bf16[1,128,512]{2,1,0:T(8,128)(2,1)} %param.12) | copy-start | bytes 393220
  96.1 7.1 %copy-start.1 = (bf16[512,3200]{1,0:T(8,128)(2,1)S(1)}, bf16[512,3200]{1,0:T(8,128)(2,1)}, u32[]{:S(2)}) copy-start(bf16[512,3200]{1,0:T(8,128)(2,1)} %get-tuple-element.11.wq) | copy-start | bytes 9830404
  148.5 17.1 %copy-start.7 = (s32[1,256]{1,0:T(1,128)S(1)}, s32[1,256]{1,0:T(1,128)}, u32[]{:S(2)}) copy-start(s32[1,256]{1,0:T(1,128)} %param.15) | copy-start | bytes 3076
  148.5 17.1 %copy-start.5 = (f32[1,1024]{1,0:T(1,128)S(1)}, f32[1,1024]{1,0:T(1,128)}, u32[]{:S(2)}) copy-start(f32[1,1024]{1,0:T(1,128)} %param.14) | copy-start | bytes 12292
Sparse Core Ops, SparseCore 0:
  165.7 115.7 reduce-scatter.1

commit v2 on v1

--- a/solution.py
+++ b/solution.py
@@ -270,29 +270,36 @@
             DMA((2, 3)), DMA((2, 3)), DMA((2, 16)), DMA((2, 16)), DMA((2, 18)), DMA((2, 18)), DMA((3,)), DMA((3,)),
         ],
         compiler_params=pltpu.CompilerParams(
-            collective_id=0, has_side_effects=True, vmem_limit_bytes=48 * 1024 * 1024
+            collective_id=0, has_side_effects=True, vmem_limit_bytes=58 * 1024 * 1024
         ),
         name="gather",
     )(pooled, w, dout, bags, slots)
 
 
 def reduce_kernel(
-    bp, wq, flat,
-    bpall, first, up_send, down_send, up_recv, down_recv, acc,
-    bsend, brecv, fsend, frecv, usend, urecv, vsend, vrecv,
+    bp, wq, counts,
+    out,
+    bpall, acc, send1, recv1, flat, cv, mate_out, mate_in, own_rows, send2, recv2, yout, yin,
+    bsend, brecv, ssem1, rsem1, csem, msend, mrecv, ssem2, rsem2, ysem,
 ):
     s, y, z, c = place()
     mate, other, diag = shard_of(y, z, 1 - c), shard_of(1 - y, z, c), shard_of(1 - y, z, 1 - c)
-    ahead, behind = shard_of(y, (z + 1) % NZ, c), shard_of(y, (z + NZ - 1) % NZ, c)
+    peers = (shard_of(y, (z + 1) % NZ, c), shard_of(y, (z + NZ - 1) % NZ, c))
     hid = bp.shape[1]
     quarter = wq.shape[1]
     rows = acc.shape[1]
-    cut = (quarter // EMB + 1) // 2 * EMB
+    samples = rows // 4
+    slabs = [(z + step) % NZ for step in (4, 3, 5, 2, 6, 1, 7, 0)]
+
+    def load_counts(n):
+        return pltpu.make_async_copy(counts.at[:, slabs[n]], cv.at[n % 4], csem.at[n % 4])
+
+    for n in range(4):
+        load_counts(n).start()
     barrier = pltpu.get_barrier_semaphore()
-    peers = (mate, other, diag, ahead, behind)
-    for peer in peers:
+    for peer in (mate, other, diag) + peers:
         pl.semaphore_signal(barrier, inc=1, device_id=shard_id(peer), device_id_type=MESH)
-    pl.semaphore_wait(barrier, len(peers))
+    pl.semaphore_wait(barrier, 5)
     me4 = pl.multiple_of((y * 2 + c) * hid, hid)
     sent = []
 
@@ -301,99 +308,157 @@
         sent.append(copy)
         return copy
 
-    got = [
+    got_bp = [
         go(remote(bp, bpall.at[:, pl.ds(me4, hid)], bsend.at[i], brecv.at[i], shard_id(peer)))
         for i, peer in enumerate((other, diag, mate))
     ]
     bpall[:, pl.ds(me4, hid)] = bp[...]
-    for copy in got:
+    flat[...] = jnp.zeros_like(flat)
+    for copy in got_bp:
         copy.wait_recv()
 
+    def ring(view, calc, own, send, recv, ssem, rsem):
+        copies = {}
+
+        def push(direction, h, part, value):
+            place_at = view(send, direction, h, part)
+            place_at[...] = value.astype(send.dtype)
+            index = h * 2 + part
+            copies[(direction, h, part)] = go(remote(
+                place_at, view(recv, direction, h, part),
+                ssem.at[direction, index], rsem.at[direction, index], shard_id(peers[direction])))
+
+        def got(direction, h, part):
+            copies[(direction, h, part)].wait_recv()
+            return view(recv, direction, h, part)[...].astype(F32)
+
+        calc(0)
+        push(0, 0, 0, own(0, 0))
+        push(1, 0, 1, own(0, 1))
+        calc(1)
+        calc(2)
+        push(0, 1, 1, own(1, 1))
+        push(1, 1, 0, own(2, 0))
+        calc(3)
+        calc(4)
+        push(0, 1, 0, own(1, 0) + got(0, 0, 0))
+        push(1, 1, 1, own(2, 1) + got(1, 0, 1))
+        calc(5)
+        calc(6)
+        for h in (2, 3):
+            n = 2 * h - 1
+            push(0, h, 1, own(n, 1) + got(0, h - 1, 1))
+            push(1, h, 0, own(n + 1, 0) + got(1, h - 1, 0))
+            push(0, h, 0, own(n, 0) + got(0, h - 1, 0))
+            push(1, h, 1, own(n + 1, 1) + got(1, h - 1, 1))
+            if h == 2:
+                calc(7)
+
+        def final(part):
+            return own(7, part) + got(0, 3, part) + got(1, 3, part)
+
+        return final
+
     tile = quarter // 5 if quarter % (5 * EMB) == 0 else EMB
-    tiles = quarter // tile
-
-    def product(slab, write):
-        left = bpall[pl.ds(pl.multiple_of(slab * rows, rows), rows), :]
+    cut = (quarter // EMB + 1) // 2 * EMB
+    spans = ((0, cut), (cut, quarter))
+
+    def product(n):
+        left = bpall[pl.ds(pl.multiple_of(slabs[n] * rows, rows), rows), :]
 
         def body(i, carry):
-            at = pl.multiple_of(i * tile, EMB)
-            write(at, jnp.dot(left, wq[:, pl.ds(at, tile)], preferred_element_type=F32))
+            at = pl.ds(pl.multiple_of(i * tile, EMB), tile)
+            acc[n % 4, :, at] = jnp.dot(left, wq[:, at], preferred_element_type=F32)
             return carry
 
-        lax.fori_loop(0, tiles, body, 0)
-
-    def into_first(at, value):
-        first[:, pl.ds(at, tile)] = value.astype(BF)
-
-    def into_acc(which):
-        def write(at, value):
-            acc[which, :, pl.ds(at, tile)] = value
-        return write
-
-    product((z + 4) % NZ, into_first)
-    arriving = [
-        go(remote(first.at[:, :cut], up_recv.at[0, :, pl.ds(0, cut)], fsend.at[0], frecv.at[0], shard_id(ahead))),
-        go(remote(first.at[:, cut:], down_recv.at[0, :, pl.ds(cut, quarter - cut)], fsend.at[1], frecv.at[1], shard_id(behind))),
-    ]
-    for k in range(3):
-        hop = 3 - k
-        product((z + hop) % NZ, into_acc(0))
-        product((z + NZ - hop) % NZ, into_acc(1))
-        arriving[0].wait_recv()
-        if k == 0:
-            up_send[k, :, :cut] = (acc[0, :, :cut] + up_recv[k, :, :cut].astype(F32)).astype(BF)
-            up_send[k, :, cut:] = acc[0, :, cut:].astype(BF)
-        else:
-            up_send[k] = (acc[0] + up_recv[k].astype(F32)).astype(BF)
-        up = go(remote(up_send.at[k], up_recv.at[k + 1], usend.at[k], urecv.at[k], shard_id(ahead)))
-        arriving[1].wait_recv()
-        if k == 0:
-            down_send[k, :, cut:] = (acc[1, :, cut:] + down_recv[k, :, cut:].astype(F32)).astype(BF)
-            down_send[k, :, :cut] = acc[1, :, :cut].astype(BF)
-        else:
-            down_send[k] = (acc[1] + down_recv[k].astype(F32)).astype(BF)
-        down = go(remote(down_send.at[k], down_recv.at[k + 1], vsend.at[k], vrecv.at[k], shard_id(behind)))
-        arriving = [up, down]
-    product(z, into_acc(0))
-    flat[...] = jnp.zeros_like(flat)
-    for copy in arriving:
-        copy.wait_recv()
-    samples = rows // 4
-    for f in range(quarter // EMB):
-        at = slice(f * EMB, (f + 1) * EMB)
-        total = acc[0, :, at] + up_recv[3, :, at].astype(F32) + down_recv[3, :, at].astype(F32)
-        total = total.astype(BF)
-        for i in range(4):
-            flat[i, f * samples:(f + 1) * samples, :] = total[i * samples:(i + 1) * samples]
+        lax.fori_loop(0, quarter // tile, body, 0)
+
+    def view1(buf, direction, h, part):
+        return buf.at[direction, h, :, spans[part][0]:spans[part][1]]
+
+    def own1(n, part):
+        return acc[n % 4, :, spans[part][0]:spans[part][1]]
+
+    final = ring(view1, product, own1, send1, recv1, ssem1, rsem1)
+    for part in (1, 0):
+        total = final(part).astype(BF)
+        for f in range(spans[part][0] // EMB, spans[part][1] // EMB):
+            at = f * EMB - spans[part][0]
+            for i in range(4):
+                flat[i, f * samples:(f + 1) * samples, :] = total[i * samples:(i + 1) * samples, at:at + EMB]
+
+    bags = flat.shape[0] * flat.shape[1]
+    mates = {}
+
+    def row_sums(n):
+        load_counts(n).wait()
+        for yy in range(2):
+            mate_out[n, yy] = jnp.dot(cv[n % 4, yy, 1 - c], flat[...].reshape(bags, EMB), preferred_element_type=F32)
+        mates[n] = go(remote(mate_out.at[n], mate_in.at[n], msend.at[n], mrecv.at[n], shard_id(mate)))
+        for yy in range(2):
+            own_rows[n, yy] = jnp.dot(cv[n % 4, yy, c], flat[...].reshape(bags, EMB), preferred_element_type=F32)
+        if n + 4 < 8:
+            load_counts(n + 4).start()
+
+    def calc2(n):
+        if n == 0:
+            row_sums(0)
+            row_sums(1)
+        elif n > 1:
+            row_sums(n)
+
+    def view2(buf, direction, h, part):
+        return buf.at[direction, h, part]
+
+    def own2(n, part):
+        if n in mates:
+            mates.pop(n).wait_recv()
+        return own_rows[n, part] + mate_in[n, part]
+
+    final = ring(view2, calc2, own2, send2, recv2, ssem2, rsem2)
+    sums = [final(0), final(1)]
+    yout[...] = jnp.where(y == 0, sums[1], sums[0])
+    last = go(remote(yout, yin, ysem.at[0], ysem.at[1], shard_id(other)))
+    mine = jnp.where(y == 0, sums[0], sums[1])
+    last.wait_recv()
+    out[...] = mine + yin[...]
     for copy in sent:
         copy.wait_send()
 
 
-def reduce_all(bp, wq, pad, samples):
+def reduce_all(bp, wq, counts, samples):
     batch, hid = bp.shape
     quarter = wq.shape[1]
     rows = 4 * samples
+    owners, touched, width = counts.shape
     vm = pl.BlockSpec(memory_space=VMEM)
     return pl.pallas_call(
         reduce_kernel,
-        out_shape=jax.ShapeDtypeStruct((4, pad, EMB), BF),
-        in_specs=[vm, vm],
+        out_shape=jax.ShapeDtypeStruct((touched, EMB), F32),
+        in_specs=[vm, vm, pl.BlockSpec(memory_space=pl.ANY)],
         out_specs=vm,
         scratch_shapes=[
             VMEM((batch, 4 * hid), BF),
-            VMEM((rows, quarter), BF),
-            VMEM((3, rows, quarter), BF),
-            VMEM((3, rows, quarter), BF),
-            VMEM((4, rows, quarter), BF),
-            VMEM((4, rows, quarter), BF),
-            VMEM((2, rows, quarter), F32),
-            DMA((3,)), DMA((3,)), DMA((2,)), DMA((2,)), DMA((3,)), DMA((3,)), DMA((3,)), DMA((3,)),
+            VMEM((4, rows, quarter), F32),
+            VMEM((2, 4, rows, quarter), BF),
+            VMEM((2, 4, rows, quarter), BF),
+            VMEM((4, width // 4, EMB), BF),
+            VMEM((4, 2, 2, touched, width), BF),
+            VMEM((8, 2, touched, EMB), F32),
+            VMEM((8, 2, touched, EMB), F32),
+            VMEM((8, 2, touched, EMB), F32),
+            VMEM((2, 4, 2, touched, EMB), F32),
+            VMEM((2, 4, 2, touched, EMB), F32),
+            VMEM((touched, EMB), F32),
+            VMEM((touched, EMB), F32),
+            DMA((3,)), DMA((3,)), DMA((2, 8)), DMA((2, 8)), DMA((4,)), DMA((8,)), DMA((8,)), DMA((2, 8)), DMA((2, 8)),
+            DMA((2,)),
         ],
         compiler_params=pltpu.CompilerParams(
-            collective_id=1, has_side_effects=True, vmem_limit_bytes=48 * 1024 * 1024
+            collective_id=1, has_side_effects=True, vmem_limit_bytes=58 * 1024 * 1024
         ),
         name="reduce",
-    )(bp, wq)
+    )(bp, wq, counts.reshape(2, NZ, 2, touched, width))
 
 
 def shards(pooled, dout, w_first, w_second, table, accum, touched_ids, lookup_bag, lookup_slot):
@@ -410,11 +475,7 @@
     hidden = (pre * sig).astype(BF)
     back_hidden = contract_last(grad_all, w_second[0])
     back_pre = (back_hidden * sig * (1.0 + pre * (1.0 - sig))).astype(BF)
-    flat = reduce_all(back_pre, wq, counts.shape[2] // 4, samples)
-    partial = jnp.dot(
-        counts.reshape(n_shard * TOUCHED, -1), flat.reshape(-1, EMB), preferred_element_type=F32
-    )
-    row_grad = lax.psum_scatter(partial, "shard", scatter_dimension=0, tiled=True)
+    row_grad = reduce_all(back_pre, wq, counts, samples)
     grad_first = contract_first(back_pre, inputs_all) * scale
     grad_second = contract_first(hidden, grad_all) * scale
     row_ids = touched_ids[0]

time: 295 us -> 183 us (0.62); the launches traced: 292 us -> 183 us
  waiting for transfers between devices: 103 us -> 0 us
  Pallas kernels: 129 us -> 157 us
  matrix products: 34.6 us -> 18.1 us
  between operations: 14.2 us -> 0.76 us
  local copies, waits for them, and re-layouts: 6.37 us -> 2.8 us
    reduce_scatter x1 -> x0, waiting for transfers between devices: 103 us -> none  [shards(): lax.psum_scatter(partial, 'shard', scatter_dimension=0, tiled=True)]
    pallas_call x1, Pallas kernels: 45.3 us -> 73.2 us  [reduce_all(): pl.pallas_call(reduce_kernel, out_shape=jax.ShapeDtypeStruct((touched, EM...]
    dot_general x1 -> x0, matrix products: 17.1 us -> none  [shards(): jnp.dot(counts.reshape(n_shard * TOUCHED, -1), flat.reshape(-1, EMB), pre...]
    unnamed x18 -> x14, local copies, waits for them, and re-layouts: 4.21 us -> 0.03 us
  transfers between devices with their start and end apart: 1 -> 0, of which waited for: 1 -> 0; matrix products, arithmetic and copies ran while one was open for 4% -> 0% of each run, Pallas kernels for 0% -> 0%
where the time goes in v2:
time: 183 us
  Pallas kernels  157 us (86%)
  matrix products  18.1 us (10%)
  other arithmetic  4.04 us (2%)
  local copies, waits for them, and re-layouts  2.8 us (2%)
    pallas_call x1, Pallas kernels, gather_all(): pl.pallas_call(gather_kernel, out_shape=(jax.ShapeDtypeStruct((n_shard, s...  83.7 us
    pallas_call x1, Pallas kernels, reduce_all(): pl.pallas_call(reduce_kernel, out_shape=jax.ShapeDtypeStruct((touched, EM...  73.2 us
    dot_general x2, matrix products, contract_first(): lax.dot_general(left, right, (((0,), (0,)), ((), ())), preferred_element_...  10.5 us
    dot_general x2, matrix products, contract_last(): lax.dot_general(left, right, (((1,), (1,)), ((), ())), preferred_element_...  7.62 us

profile of v2, /device:TPU:1, one launch (start us, length us, event | category | flops | bytes accessed | tf_op | source)
XLA Modules:
  0.0 182.7 jit_solution(11672542578061347292)
XLA Ops:
  0.6 0.0 copy-start
  0.6 0.8 convert_bitcast_fusion
  1.5 0.6 reshape.82.dout
  2.1 0.0 copy-start.2
  2.1 83.7 %gather.13 = (bf16[32,16,12800]{2,1,0:T(8,128)(2,1)}, bf16[32,16,512]{2,1,0:T(8,128)(2,1)}, bf16[512,3200]{1,0:T(8,128)(2,1)}, bf16[32,256,2048]{2,1,0:T(8,128)(2,1)}) custom-call(bf16[16,12800]{1,0:T(8,128)(2,1)} %bitcast.39, bf16[128,12800]{1,0:T(8,128)(2,1)} %bitcast.36, f32[8,8,128]{2,1,0:T(8,128)} %reshape.82.dout, s32[32,32,400]{2,1,0:T(8,128)} %bitcast.37, ...), custom_call_target="tpu_custom_call" | custom-call | tf_op jit(solution)/shard_map/gather/pallas_call | solution.py:253
  85.9 0.0 copy-done.2
  85.9 0.0 copy-start.5
  85.9 0.0 copy-start.6
  85.9 6.7 %fusion.6 = f32[512,128]{1,0:T(8,128)S(1)} fusion(bf16[512,12800]{1,0:T(8,128)(2,1)} %bitcast.34, bf16[1,128,12800]{2,1,0:T(8,128)(2,1)S(1)} %copy-done.2), kind=kOutput, calls=%fused_computation.20 | convolution fusion | flops 1677721600 | bytes 16646144 | tf_op jit(solution)/shard_map/dot_general | solution.py:24
  92.5 0.0 copy-done.5
  92.6 0.0 copy-done.6
  92.6 1.0 fusion.3.bp
  93.5 0.0 copy-start.4
  93.5 0.0 copy-start.1
  93.5 0.0 copy-start.3
  93.5 73.2 %reduce.1 = f32[256,128]{1,0:T(8,128)} custom-call(bf16[512,128]{1,0:T(8,128)(2,1)} %fusion.3.bp, bf16[512,3200]{1,0:T(8,128)(2,1)} %get-tuple-element.10.wq, bf16[2,8,2,256,2048]{4,3,2,1,0:T(8,128)(2,1)} %bitcast.33), custom_call_target="tpu_custom_call" | custom-call | tf_op jit(solution)/shard_map/reduce/pallas_call | solution.py:435
  166.8 1.0 multiply_reduce_fusion
  167.8 0.0 copy-done.4
  167.8 0.0 copy-done.1
  167.8 1.4 gather_fusion.1
  169.2 0.6 sqrt_add_fusion
  169.8 0.0 copy-done
  169.8 0.7 gather_fusion
  170.5 1.7 subtract_bitcast_fusion
  172.2 0.0 copy-done.3
  172.2 9.5 %fusion = f32[1,128,12800]{2,1,0:T(8,128)} fusion(bf16[512,128]{1,0:T(8,128)(2,1)S(1)} %copy-done.3, bf16[512,12800]{1,0:T(8,128)(2,1)} %bitcast.35), kind=kOutput, calls=%fused_computation.3 | convolution fusion | flops 1679360000 | bytes 19791872 | tf_op jit(solution)/shard_map/dot_general | solution.py:20
  181.7 1.0 fusion.1
  (3 shorter events, 0.0 us)
Async XLA Ops:
  0.6 169.1 %copy-start = (f32[1,1024,128]{2,1,0:T(8,128)S(1)}, f32[1,1024,128]{2,1,0:T(8,128)}, u32[]{:S(2)}) copy-start(f32[1,1024,128]{2,1,0:T(8,128)} %param.13) | copy-start | bytes 1572868
  2.1 83.8 %copy-start.2 = (bf16[1,128,12800]{2,1,0:T(8,128)(2,1)S(1)}, bf16[1,128,12800]{2,1,0:T(8,128)(2,1)}, u32[]{:S(2)}) copy-start(bf16[1,128,12800]{2,1,0:T(8,128)(2,1)} %param.11) | copy-start | bytes 9830404
  85.9 6.7 %copy-start.5 = (bf16[32,16,512]{2,1,0:T(8,128)(2,1)S(1)}, bf16[32,16,512]{2,1,0:T(8,128)(2,1)}, u32[]{:S(2)}) copy-start(bf16[32,16,512]{2,1,0:T(8,128)(2,1)} %get-tuple-element.8) | copy-start | bytes 1572868
  85.9 6.7 %copy-start.6 = (bf16[1,128,512]{2,1,0:T(8,128)(2,1)S(1)}, bf16[1,128,512]{2,1,0:T(8,128)(2,1)}, u32[]{:S(2)}) copy-start(bf16[1,128,512]{2,1,0:T(8,128)(2,1)} %param.12) | copy-start | bytes 393220
  93.5 74.3 %copy-start.4 = (s32[1,256]{1,0:T(1,128)S(1)}, s32[1,256]{1,0:T(1,128)}, u32[]{:S(2)}) copy-start(s32[1,256]{1,0:T(1,128)} %param.15) | copy-start | bytes 3076
  93.5 74.3 %copy-start.1 = (f32[1,1024]{1,0:T(1,128)S(1)}, f32[1,1024]{1,0:T(1,128)}, u32[]{:S(2)}) copy-start(f32[1,1024]{1,0:T(1,128)} %param.14) | copy-start | bytes 12292
  93.5 78.6 %copy-start.3 = (bf16[512,128]{1,0:T(8,128)(2,1)S(1)}, bf16[512,128]{1,0:T(8,128)(2,1)}, u32[]{:S(2)}) copy-start(bf16[512,128]{1,0:T(8,128)(2,1)} %fusion.3.bp) | copy-start | bytes 393220

commit v3 on v2

v3 whole, which is shorter than its diff:
```python
import jax
import jax.numpy as jnp
from jax import lax
from jax.experimental import pallas as pl
from jax.experimental.pallas import tpu as pltpu
from jax.sharding import PartitionSpec as P

EMB = 128
FEAT = 100
TOUCHED = 256
MESH = pl.DeviceIdType.MESH
VMEM = pltpu.VMEM
DMA = pltpu.SemaphoreType.DMA
NZ = 8
BF = jnp.bfloat16
F32 = jnp.float32


def contract_first(left, right):
    return lax.dot_general(left, right, (((0,), (0,)), ((), ())), preferred_element_type=F32)


def contract_last(left, right):
    return lax.dot_general(left, right, (((1,), (1,)), ((), ())), preferred_element_type=F32)


def place():
    s = lax.axis_index("shard")
    return s, s // 16, (s // 2) % NZ, s % 2


def shard_of(y, z, c):
    return y * 16 + z * 2 + c


def shard_id(s):
    return {"shard": s}


def remote(src, dst, send, recv, where):
    return pltpu.make_async_remote_copy(
        src_ref=src, dst_ref=dst, send_sem=send, recv_sem=recv, device_id=where, device_id_type=MESH
    )


def tower_kernel(
    pooled, w, w2, dout, bags, slots,
    big, counts, gall, bp_out, hid_out, out,
    bag_v, slot_v, dgot, stage, w_v, xblk, wq,
    bpall, acc, send1, recv1, flat, cv, mate_out, mate_in, own_rows, send2, recv2, yout, yin,
    in_sem, dsend, drecv, loc_sem, out_sem, xsem,
    first_send, first_recv, ring_send, ring_recv, mate_send, mate_recv, wsend, wrecv,
    bsend, brecv, ssem1, rsem1, csem, msend, mrecv, ssem2, rsem2, ysem,
):
    t = lax.axis_index("tower")
    s, y, z, c = place()
    towers = dout.shape[0]
    samples, cols = pooled.shape
    hid = w.shape[0]
    quarter = wq.shape[1]
    half = cols // 2
    rows = 4 * samples
    mate, other, diag = shard_of(y, z, 1 - c), shard_of(1 - y, z, c), shard_of(1 - y, z, 1 - c)
    ahead, behind = shard_of(y, (z + 1) % NZ, c), shard_of(y, (z + NZ - 1) % NZ, c)
    peers = (ahead, behind)
    me4 = y * 2 + c
    me_hid = pl.multiple_of(me4 * hid, hid)

    load_w = pltpu.make_async_copy(w, w_v, in_sem.at[2])
    load_bags = pltpu.make_async_copy(bags, bag_v, in_sem.at[0])
    load_slots = pltpu.make_async_copy(slots, slot_v, in_sem.at[1])
    load_bags.start()
    load_slots.start()
    load_w.start()

    barrier = pltpu.get_barrier_semaphore()
    for peer in (mate, other, diag, ahead, behind):
        pl.semaphore_signal(barrier, inc=1, device_id=shard_id(peer), device_id_type=MESH)
    for step in range(1, towers):
        pl.semaphore_signal(barrier, inc=1, device_id={"tower": (t + step) % towers}, device_id_type=MESH)
    pl.semaphore_wait(barrier, 5 + towers - 1)

    sent = []

    def block(zz, yy):
        return zz * 4 + yy * 2 + c

    def go(copy):
        copy.start()
        sent.append(copy)
        return copy

    mine = block(z, y)
    pending = {}

    def note(label, copy):
        pending.setdefault(label, []).append(copy)

    tile_rows = dout.shape[1]
    land = dgot.at[pl.ds(pl.multiple_of(t * tile_rows, tile_rows), tile_rows), :]
    dcopies = []
    for step in range(1, towers):
        u = (t + step) % towers
        dcopies.append(go(remote(dout.at[u], land, dsend.at[step], drecv.at[step], {"tower": u})))
    own_d = pltpu.make_async_copy(dout.at[t], land, loc_sem.at[0])
    own_d.start()

    firsts = []
    for i, peer in enumerate((ahead, behind, other)):
        firsts.append(go(remote(pooled, big.at[mine], first_send.at[0, i], first_recv.at[0, i], shard_id(peer))))
    note(0, go(remote(pooled, big.at[mine], mate_send.at[0, 0], mate_recv.at[0, 0], shard_id(mate))))
    own_p = pltpu.make_async_copy(pooled, big.at[mine], loc_sem.at[1])
    own_p.start()

    own_d.wait()
    for copy in dcopies:
        copy.wait_recv()
    per = gall.shape[2] // EMB
    for k in range(per):
        gall[mine, :, k * EMB:(k + 1) * EMB] = dgot[pl.ds(k, samples, stride=per), :].astype(BF)
    gmine = gall.at[mine]
    for i, peer in enumerate((ahead, behind, other)):
        firsts.append(go(remote(gmine, gmine, first_send.at[1, i], first_recv.at[1, i], shard_id(peer))))
    note(0, go(remote(gmine, gmine, mate_send.at[1, 0], mate_recv.at[1, 0], shard_id(mate))))

    def view(kind, at):
        if kind == 0:
            return big.at[at]
        if kind == 1:
            return gall.at[at]
        return big.at[at, :, pl.ds((kind - 2) * half, half)]

    mate_slot = [1, 1]

    def to_mate(kind, at, label):
        row = 1 if kind == 1 else 0
        slot = mate_slot[row]
        mate_slot[row] += 1
        note(label, go(remote(
            view(kind, at), view(kind, at), mate_send.at[row, slot], mate_recv.at[row, slot], shard_id(mate))))

    ring_copies = {}

    def to_ring(kind, at, hop, direction, chain):
        row = 1 if kind == 1 else 0
        index = (hop - 1) * 4 + direction * 2 + chain
        ring_copies[(row, hop, direction, chain)] = go(remote(
            view(kind, at), view(kind, at), ring_send.at[row, index], ring_recv.at[row, index],
            shard_id(peers[direction])))

    yblock = block(z, 1 - y)
    firsts[2].wait_recv()
    for direction in range(2):
        to_ring(0, yblock, 1, direction, 1)
    to_mate(0, yblock, 0)
    firsts[5].wait_recv()
    for direction in range(2):
        to_ring(1, yblock, 1, direction, 1)
    to_mate(1, yblock, 0)

    wcopies = []
    for i, (yy, cc, peer) in enumerate(((y, 1 - c, mate), (1 - y, c, other), (1 - y, 1 - c, diag))):
        part = pl.multiple_of((yy * 2 + cc) * quarter, EMB)
        wcopies.append(go(remote(
            w.at[:, pl.ds(part, quarter)], wq.at[pl.ds(me_hid, hid), :], wsend.at[i], wrecv.at[i], shard_id(peer))))
    own_w = pltpu.make_async_copy(
        w.at[:, pl.ds(pl.multiple_of(me4 * quarter, EMB), quarter)], wq.at[pl.ds(me_hid, hid), :], loc_sem.at[3])
    own_w.start()

    load_bags.wait()
    load_slots.wait()
    load_w.wait()
    look = bags.shape[2]
    pad = stage.shape[2] // 4
    local_feat = quarter // EMB
    low = me4 * local_feat

    def owner_counts(owner, slot_at):
        @pl.when(owner >= 2)
        def _():
            pltpu.make_async_copy(stage.at[slot_at], counts.at[owner], out_sem.at[slot_at]).wait()

        for i in range(4):
            source = shard_of(i // 2, z, i % 2)
            bag = bag_v[owner, pl.ds(source, 1), :]
            slot = slot_v[owner, pl.ds(source, 1), :]
            sample = (bag * 5243) >> 19
            feat = bag - sample * FEAT - low
            ok = (feat >= 0) & (feat < local_feat)
            bag_local = jnp.where(ok, feat * samples + sample, -1)
            left = (lax.broadcasted_iota(jnp.int32, (TOUCHED, look), 0) == slot).astype(F32).astype(BF)
            right = (lax.broadcasted_iota(jnp.int32, (pad, look), 0) == bag_local).astype(F32).astype(BF)
            stage[slot_at, :, i * pad:(i + 1) * pad] = contract_last(left, right).astype(BF)
        pltpu.make_async_copy(stage.at[slot_at], counts.at[owner], out_sem.at[slot_at]).start()

    owners = bags.shape[0]
    done = [0]

    def count_some(pairs):
        start = done[0]
        done[0] += pairs

        def body(p, carry):
            owner_counts(p * 2, 0)
            owner_counts(p * 2 + 1, 1)
            return carry

        lax.fori_loop(start, start + pairs, body, 0)

    def load_slab(label, zz, at):
        for copy in pending.pop(label):
            copy.wait_recv()
        load = pltpu.make_async_copy(big.at[pl.ds(zz * 4, 4)], xblk.at[at], xsem.at[at])
        load.start()
        return load

    bp_copies = {}
    step_k = cols // 10 if cols % (10 * EMB) == 0 else EMB

    def tower_step(loads, zs, names):
        m = len(zs)
        for load in loads:
            load.wait()

        def body(i, total):
            at = pl.ds(pl.multiple_of(i * step_k, EMB), step_k)
            left = xblk[0:m, :, :, at].reshape(m * rows, step_k)
            return total + contract_last(left, w_v[:, at])

        pre = lax.fori_loop(0, cols // step_k, body, jnp.zeros((m * rows, hid), F32))
        sig = jax.nn.sigmoid(pre)
        hidden = (pre * sig).astype(BF)
        for i, zz in enumerate(zs):
            part = slice(i * rows, (i + 1) * rows)
            at = pl.ds(pl.multiple_of(zz * rows, rows), rows)
            grads = gall[pl.ds(zz * 4, 4)].reshape(rows, gall.shape[2])
            back_hidden = contract_last(grads, w2[...])
            sg, p = sig[part], pre[part]
            back_pre = (back_hidden * sg * (1.0 + p * (1.0 - sg))).astype(BF)
            hid_out[at, :] = hidden[part]
            bp_out[at, :] = back_pre
            bpall[at, pl.ds(me_hid, hid)] = back_pre
            where = bpall.at[at, pl.ds(me_hid, hid)]
            bp_copies[names[i]] = [
                go(remote(where, where, bsend.at[names[i], j], brecv.at[names[i], j], shard_id(peer)))
                for j, peer in enumerate((other, diag, mate))
            ]

    steps = (4, 3, 5, 2, 6, 1, 7, 0)
    slabs = [(z + step) % NZ for step in steps]
    tile = quarter // 5 if quarter % (5 * EMB) == 0 else EMB
    cut = (quarter // EMB + 1) // 2 * EMB
    spans = ((0, cut), (cut, quarter))
    slab_w = list(wcopies)

    def product(n):
        while slab_w:
            slab_w.pop().wait_recv()
        for copy in bp_copies.pop(steps[n]):
            copy.wait_recv()
        left = bpall[pl.ds(pl.multiple_of(slabs[n] * rows, rows), rows), :]

        def body(i, carry):
            at = pl.ds(pl.multiple_of(i * tile, EMB), tile)
            acc[n % 4, :, at] = jnp.dot(left, wq[:, at], preferred_element_type=F32)
            return carry

        lax.fori_loop(0, quarter // tile, body, 0)

    count_some(3)
    own_p.wait()
    loads = [load_slab(0, z, 0)]
    zs, names = [z], [0]
    for hop in range(1, 4):
        for chain in range(2):
            if chain == 1:
                tower_step(loads, zs, names)
            count_some(2)
            yy = y if chain == 0 else 1 - y
            for direction in range(2):
                zz = (z + hop) % NZ if direction else (z + NZ - hop) % NZ
                at = block(zz, yy)
                label = (hop, direction)
                if hop == 1 and chain == 0:
                    firsts[direction].wait_recv()
                else:
                    ring_copies[(0, hop, direction, chain)].wait_recv()
                to_ring(0 if hop < 3 else 2 + direction, at, hop + 1, direction, chain)
                to_mate(0, at, label)
                if hop == 1 and chain == 0:
                    firsts[3 + direction].wait_recv()
                else:
                    ring_copies[(1, hop, direction, chain)].wait_recv()
                if hop < 3 or direction == 0:
                    to_ring(1, at, hop + 1, direction, chain)
                to_mate(1, at, label)
        if hop == 3:
            count_some(1)
        zs = [(z + NZ - hop) % NZ, (z + hop) % NZ]
        names = [NZ - hop, hop]
        loads = [load_slab((hop, direction), zs[direction], direction) for direction in range(2)]
    own_w.wait()
    tower_step(loads, zs, names)
    for slot_at in range(2):
        pltpu.make_async_copy(stage.at[slot_at], counts.at[owners - 2 + slot_at], out_sem.at[slot_at]).wait()

    depth = cv.shape[0]
    grid = counts.reshape(2, NZ, 2, TOUCHED, 4 * pad)

    def load_counts(n):
        return pltpu.make_async_copy(grid.at[:, slabs[n]], cv.at[n % depth], csem.at[n % depth])

    for n in range(depth):
        load_counts(n).start()
    flat[...] = jnp.zeros_like(flat)
    product(1)
    product(2)
    zz = (z + 4) % NZ
    for chain in range(2):
        yy = y if chain == 0 else 1 - y
        at = block(zz, yy)
        for direction in range(2):
            ring_copies[(0, 4, direction, chain)].wait_recv()
            to_mate(2 + direction, at, 4)
        ring_copies[(1, 4, 0, chain)].wait_recv()
        to_mate(1, at, 4)

    def ring(view, calc, own, send, recv, ssem, rsem, early):
        copies = {}

        def push(direction, h, part, value):
            place_at = view(send, direction, h, part)
            place_at[...] = value.astype(send.dtype)
            index = h * 2 + part
            copies[(direction, h, part)] = go(remote(
                place_at, view(recv, direction, h, part),
                ssem.at[direction, index], rsem.at[direction, index], shard_id(peers[direction])))

        def got(direction, h, part):
            copies[(direction, h, part)].wait_recv()
            return view(recv, direction, h, part)[...].astype(F32)

        if early:
            push(0, 1, 1, own(1, 1))
            push(1, 1, 0, own(2, 0))
        calc(0)
        push(0, 0, 0, own(0, 0))
        push(1, 0, 1, own(0, 1))
        if not early:
            calc(1)
            calc(2)
            push(0, 1, 1, own(1, 1))
            push(1, 1, 0, own(2, 0))
        calc(3)
        calc(4)
        push(0, 1, 0, own(1, 0) + got(0, 0, 0))
        push(1, 1, 1, own(2, 1) + got(1, 0, 1))
        calc(5)
        calc(6)
        for h in (2, 3):
            n = 2 * h - 1
            push(0, h, 1, own(n, 1) + got(0, h - 1, 1))
            push(1, h, 0, own(n + 1, 0) + got(1, h - 1, 0))
            push(0, h, 0, own(n, 0) + got(0, h - 1, 0))
            push(1, h, 1, own(n + 1, 1) + got(1, h - 1, 1))
            if h == 2:
                calc(7)

        def final(part):
            return own(7, part) + got(0, 3, part) + got(1, 3, part)

        return final

    def view1(buf, direction, h, part):
        return buf.at[direction, h, :, spans[part][0]:spans[part][1]]

    def own1(n, part):
        return acc[n % 4, :, spans[part][0]:spans[part][1]]

    def calc1(n):
        if n == 0:
            tower_step([load_slab(4, zz, 0)], [zz], [4])
        product(n)

    final = ring(view1, calc1, own1, send1, recv1, ssem1, rsem1, True)
    for part in (1, 0):
        total = final(part).astype(BF)
        for f in range(spans[part][0] // EMB, spans[part][1] // EMB):
            at = f * EMB - spans[part][0]
            for i in range(4):
                flat[i, f * samples:(f + 1) * samples, :] = total[i * samples:(i + 1) * samples, at:at + EMB]

    local_bags = flat.shape[0] * flat.shape[1]
    mates = {}

    def row_sums(n):
        load_counts(n).wait()
        for yy in range(2):
            mate_out[n, yy] = jnp.dot(
                cv[n % depth, yy, 1 - c], flat[...].reshape(local_bags, EMB), preferred_element_type=F32)
        mates[n] = go(remote(mate_out.at[n], mate_in.at[n], msend.at[n], mrecv.at[n], shard_id(mate)))
        for yy in range(2):
            own_rows[n, yy] = jnp.dot(
                cv[n % depth, yy, c], flat[...].reshape(local_bags, EMB), preferred_element_type=F32)
        if n + depth < NZ:
            load_counts(n + depth).start()

    def calc2(n):
        if n == 0:
            row_sums(0)
            row_sums(1)
        elif n > 1:
            row_sums(n)

    def view2(buf, direction, h, part):
        return buf.at[direction, h, part]

    def own2(n, part):
        if n in mates:
            mates.pop(n).wait_recv()
        return own_rows[n, part] + mate_in[n, part]

    final = ring(view2, calc2, own2, send2, recv2, ssem2, rsem2, False)
    sums = [final(0), final(1)]
    yout[...] = jnp.where(y == 0, sums[1], sums[0])
    last = go(remote(yout, yin, ysem.at[0], ysem.at[1], shard_id(other)))
    kept = jnp.where(y == 0, sums[0], sums[1])
    last.wait_recv()
    out[...] = kept + yin[...]
    for copy in sent:
        copy.wait_send()


def tower_all(pooled, w, w2, dout, bags, slots):
    samples, cols = pooled.shape
    hid = w.shape[0]
    n_shard = bags.shape[0]
    batch = n_shard * samples
    out = w2.shape[1]
    quarter = cols // 4
    rows = 4 * samples
    pad = -(-(quarter // EMB * samples) // 512) * 512
    any_spec = pl.BlockSpec(memory_space=pl.ANY)
    vm = pl.BlockSpec(memory_space=VMEM)
    depth = 3
    return pl.pallas_call(
        tower_kernel,
        out_shape=(
            jax.ShapeDtypeStruct((n_shard, samples, cols), BF),
            jax.ShapeDtypeStruct((n_shard, TOUCHED, 4 * pad), BF),
            jax.ShapeDtypeStruct((n_shard, samples, out), BF),
            jax.ShapeDtypeStruct((batch, hid), BF),
            jax.ShapeDtypeStruct((batch, hid), BF),
            jax.ShapeDtypeStruct((TOUCHED, EMB), F32),
        ),
        in_specs=[any_spec, any_spec, vm, any_spec, any_spec, any_spec],
        out_specs=(any_spec, any_spec, vm, vm, vm, vm),
        scratch_shapes=[
            VMEM(bags.shape, jnp.int32),
            VMEM(slots.shape, jnp.int32),
            VMEM((dout.shape[0] * dout.shape[1], EMB), F32),
            VMEM((2, TOUCHED, 4 * pad), BF),
            VMEM((hid, cols), BF),
            VMEM((2, 4, samples, cols), BF),
            VMEM((4 * hid, quarter), BF),
            VMEM((batch, 4 * hid), BF),
            VMEM((4, rows, quarter), F32),
            VMEM((2, 4, rows, quarter), BF),
            VMEM((2, 4, rows, quarter), BF),
            VMEM((4, pad, EMB), BF),
            VMEM((depth, 2, 2, TOUCHED, 4 * pad), BF),
            VMEM((NZ, 2, TOUCHED, EMB), F32),
            VMEM((NZ, 2, TOUCHED, EMB), F32),
            VMEM((NZ, 2, TOUCHED, EMB), F32),
            VMEM((2, 4, 2, TOUCHED, EMB), F32),
            VMEM((2, 4, 2, TOUCHED, EMB), F32),
            VMEM((TOUCHED, EMB), F32),
            VMEM((TOUCHED, EMB), F32),
            DMA((3,)), DMA((8,)), DMA((8,)), DMA((4,)), DMA((2,)), DMA((2,)),
            DMA((2, 3)), DMA((2, 3)), DMA((2, 16)), DMA((2, 16)), DMA((2, 18)), DMA((2, 18)), DMA((3,)), DMA((3,)),
            DMA((8, 3)), DMA((8, 3)), DMA((2, 8)), DMA((2, 8)), DMA((depth,)), DMA((8,)), DMA((8,)),
            DMA((2, 8)), DMA((2, 8)), DMA((2,)),
        ],
        compiler_params=pltpu.CompilerParams(
            collective_id=0, has_side_effects=True, vmem_limit_bytes=60 * 1024 * 1024
        ),
        name="tower",
    )(pooled, w, w2, dout, bags, slots)


def shards(pooled, dout, w_first, w_second, table, accum, touched_ids, lookup_bag, lookup_slot):
    towers = dout.shape[1]
    samples = pooled.shape[1]
    dtiles = jnp.transpose(dout, (1, 0, 2)).astype(F32).reshape(towers, -1, EMB)
    big, _, gall, back_pre, hidden, row_grad = tower_all(
        pooled[0], w_first[0], w_second[0], dtiles, lookup_bag[0], lookup_slot[0])
    n_shard = big.shape[0]
    inputs_all = big.reshape(n_shard * samples, -1)
    grad_all = gall.reshape(n_shard * samples, -1)
    scale = float(samples * n_shard) ** (-0.5)
    grad_first = contract_first(back_pre, inputs_all) * scale
    grad_second = contract_first(hidden, grad_all) * scale
    row_ids = touched_ids[0]
    old_rows = table[0][row_ids]
    old_acc = accum[0][row_ids]
    new_acc = old_acc + jnp.mean(row_grad * row_grad, axis=-1)
    new_row = old_rows - 0.5 * row_grad / (jnp.sqrt(new_acc)[:, None] + 1e-08)
    return (grad_first[None], grad_second[None], new_row[None], new_acc[None])


def solution(mesh):
    in_specs = (
        P("tower", "shard", None),
        P(("tower", "shard"), None, None),
        P("tower", "shard", None),
        P("tower", "shard", None),
        P("tower", "shard", None),
        P("tower", "shard"),
        P("tower", "shard"),
        P("tower", None, None, None),
        P("tower", None, None, None),
    )
    out_specs = (
        P("tower", "shard", None),
        P("tower", "shard", None),
        P("tower", "shard", None),
        P("tower", "shard"),
    )
    return jax.shard_map(shards, mesh=mesh, in_specs=in_specs, out_specs=out_specs, check_vma=False)
```

time: 183 us -> 176 us (0.962)
  matrix products: 18.1 us -> 11.6 us
    dot_general x2 -> x0, matrix products: 7.62 us -> none  [contract_last(): lax.dot_general(left, right, (((1,), (1,)), ((), ())), preferred_element_...]
    pallas_call x2 -> x1, Pallas kernels: 157 us -> 156 us  [tower_all(): pl.pallas_call(tower_kernel, out_shape=(jax.ShapeDtypeStruct((n_shard, sa...]
where the time goes in v3:
time: 176 us
  Pallas kernels  156 us (89%)
  matrix products  11.6 us (7%)
  other arithmetic  4.03 us (2%)
  local copies, waits for them, and re-layouts  2.79 us (2%)
    pallas_call x1, Pallas kernels, tower_all(): pl.pallas_call(tower_kernel, out_shape=(jax.ShapeDtypeStruct((n_shard, sa...  156 us
    dot_general x2, matrix products, contract_first(): lax.dot_general(left, right, (((0,), (0,)), ((), ())), preferred_element_...  11.6 us

profile of v3, /device:TPU:1, one launch (start us, length us, event | category | flops | bytes accessed | tf_op | source)
XLA Modules:
  0.0 175.6 jit_solution(5502672583442610000)
XLA Ops:
  0.6 0.0 copy-start
  0.6 0.0 copy-start.2
  0.7 0.0 copy-start.1
  0.7 0.8 convert_bitcast_fusion
  1.5 0.6 reshape.78.dout
  2.1 156.4 %tower.1 = (bf16[32,16,12800]{2,1,0:T(8,128)(2,1)}, bf16[32,256,2048]{2,1,0:T(8,128)(2,1)}, bf16[32,16,512]{2,1,0:T(8,128)(2,1)}, bf16[512,128]{1,0:T(8,128)(2,1...) custom-call(bf16[16,12800]{1,0:T(8,128)(2,1)} %bitcast.32, bf16[128,12800]{1,0:T(8,128)(2,1)} %bitcast.28, ...), custom_call_target="tpu_custom_call" | custom-call | tf_op jit(solution)/shard_map/tower/pallas_call | solution.py:446
  158.6 1.0 multiply_reduce_fusion
  159.6 0.0 copy-done.2
  159.6 0.0 copy-done.1
  159.6 1.4 gather_fusion.1
  161.0 0.6 sqrt_add_fusion
  161.6 0.0 copy-done
  161.6 0.7 gather_fusion
  162.3 1.7 subtract_bitcast_fusion
  164.0 2.1 %fusion.1 = f32[1,128,512]{2,1,0:T(8,128)} fusion(bf16[512,128]{1,0:T(8,128)(2,1)} %get-tuple-element.11, bf16[512,512]{1,0:T(8,128)(2,1)} %bitcast.31), kind=kOutput, calls=%fused_computation.5 | convolution fusion | flops 67174400 | bytes 917504 | tf_op jit(solution)/shard_map/dot_general | solution.py:20
  166.0 9.6 %fusion = f32[1,128,12800]{2,1,0:T(8,128)} fusion(bf16[512,128]{1,0:T(8,128)(2,1)} %get-tuple-element.9, bf16[512,12800]{1,0:T(8,128)(2,1)} %bitcast.27), kind=kOutput, calls=%fused_computation.3 | convolution fusion | flops 1679360000 | bytes 19791872 | tf_op jit(solution)/shard_map/dot_general | solution.py:20
  (3 shorter events, 0.0 us)
Async XLA Ops:
  0.6 160.9 %copy-start = (f32[1,1024,128]{2,1,0:T(8,128)S(1)}, f32[1,1024,128]{2,1,0:T(8,128)}, u32[]{:S(2)}) copy-start(f32[1,1024,128]{2,1,0:T(8,128)} %param.13) | copy-start | bytes 1572868
  0.6 158.9 %copy-start.2 = (s32[1,256]{1,0:T(1,128)S(1)}, s32[1,256]{1,0:T(1,128)}, u32[]{:S(2)}) copy-start(s32[1,256]{1,0:T(1,128)} %param.15) | copy-start | bytes 3076
  0.7 159.0 %copy-start.1 = (f32[1,1024]{1,0:T(1,128)S(1)}, f32[1,1024]{1,0:T(1,128)}, u32[]{:S(2)}) copy-start(f32[1,1024]{1,0:T(1,128)} %param.14) | copy-start | bytes 12292

commit v4 on v3

--- a/solution.py
+++ b/solution.py
@@ -472,8 +472,8 @@
             VMEM((NZ, 2, TOUCHED, EMB), F32),
             VMEM((NZ, 2, TOUCHED, EMB), F32),
             VMEM((NZ, 2, TOUCHED, EMB), F32),
-            VMEM((2, 4, 2, TOUCHED, EMB), F32),
-            VMEM((2, 4, 2, TOUCHED, EMB), F32),
+            VMEM((2, 4, 2, TOUCHED, EMB), BF),
+            VMEM((2, 4, 2, TOUCHED, EMB), BF),
             VMEM((TOUCHED, EMB), F32),
             VMEM((TOUCHED, EMB), F32),
             DMA((3,)), DMA((8,)), DMA((8,)), DMA((4,)), DMA((2,)), DMA((2,)),

time: 176 us -> 171 us (0.972)
  Pallas kernels: 156 us -> 151 us
    pallas_call x1, Pallas kernels: 156 us -> 151 us  [tower_all(): pl.pallas_call(tower_kernel, out_shape=(jax.ShapeDtypeStruct((n_shard, sa...]
where the time goes in v4:
time: 171 us; the launch traced here: 170 us
  Pallas kernels  151 us (88%)
  matrix products  11.6 us (7%)
  other arithmetic  4.03 us (2%)
  local copies, waits for them, and re-layouts  2.78 us (2%)
    pallas_call x1, Pallas kernels, tower_all(): pl.pallas_call(tower_kernel, out_shape=(jax.ShapeDtypeStruct((n_shard, sa...  151 us
    dot_general x2, matrix products, contract_first(): lax.dot_general(left, right, (((0,), (0,)), ((), ())), preferred_element_...  11.6 us

profile of v4, /device:TPU:1, one launch (start us, length us, event | category | flops | bytes accessed | tf_op | source)
XLA Modules:
  0.0 170.2 jit_solution(7939928142175317814)
XLA Ops:
  0.6 0.0 copy-start
  0.6 0.0 copy-start.2
  0.7 0.0 copy-start.1
  0.7 0.8 convert_bitcast_fusion
  1.5 0.6 reshape.78.dout
  2.1 151.1 %tower.1 = (bf16[32,16,12800]{2,1,0:T(8,128)(2,1)}, bf16[32,256,2048]{2,1,0:T(8,128)(2,1)}, bf16[32,16,512]{2,1,0:T(8,128)(2,1)}, bf16[512,128]{1,0:T(8,128)(2,1...) custom-call(bf16[16,12800]{1,0:T(8,128)(2,1)} %bitcast.32, bf16[128,12800]{1,0:T(8,128)(2,1)} %bitcast.28, ...), custom_call_target="tpu_custom_call" | custom-call | tf_op jit(solution)/shard_map/tower/pallas_call | solution.py:446
  153.2 1.0 multiply_reduce_fusion
  154.2 0.0 copy-done.2
  154.2 0.0 copy-done.1
  154.3 1.4 gather_fusion.1
  155.6 0.6 sqrt_add_fusion
  156.2 0.0 copy-done
  156.2 0.7 gather_fusion
  156.9 1.7 subtract_bitcast_fusion
  158.6 2.1 %fusion.1 = f32[1,128,512]{2,1,0:T(8,128)} fusion(bf16[512,128]{1,0:T(8,128)(2,1)} %get-tuple-element.11, bf16[512,512]{1,0:T(8,128)(2,1)} %bitcast.31), kind=kOutput, calls=%fused_computation.5 | convolution fusion | flops 67174400 | bytes 917504 | tf_op jit(solution)/shard_map/dot_general | solution.py:20
  160.7 9.6 %fusion = f32[1,128,12800]{2,1,0:T(8,128)} fusion(bf16[512,128]{1,0:T(8,128)(2,1)} %get-tuple-element.9, bf16[512,12800]{1,0:T(8,128)(2,1)} %bitcast.27), kind=kOutput, calls=%fused_computation.3 | convolution fusion | flops 1679360000 | bytes 19791872 | tf_op jit(solution)/shard_map/dot_general | solution.py:20
  (3 shorter events, 0.0 us)
Async XLA Ops:
  0.6 155.6 %copy-start = (f32[1,1024,128]{2,1,0:T(8,128)S(1)}, f32[1,1024,128]{2,1,0:T(8,128)}, u32[]{:S(2)}) copy-start(f32[1,1024,128]{2,1,0:T(8,128)} %param.13) | copy-start | bytes 1572868
  0.6 153.6 %copy-start.2 = (s32[1,256]{1,0:T(1,128)S(1)}, s32[1,256]{1,0:T(1,128)}, u32[]{:S(2)}) copy-start(s32[1,256]{1,0:T(1,128)} %param.15) | copy-start | bytes 3076
  0.7 153.6 %copy-start.1 = (f32[1,1024]{1,0:T(1,128)S(1)}, f32[1,1024]{1,0:T(1,128)}, u32[]{:S(2)}) copy-start(f32[1,1024]{1,0:T(1,128)} %param.14) | copy-start | bytes 12292
